TPU v7x, 32 devices: a whole 2x2x4 slice. The times are simulated.
32 devices in a mesh: dp: 8 (over y, x, core), tensor: 4 (over z).
Axes of the slice: x: 2, y: 2, z: 4, core: 2. Of those that a mesh axis runs over, the one named last changes fastest.
Arguments:
- inputs: bfloat16 [16384, 1024], P('dp'), may hold values from -6 to 6
- cotangent: bfloat16 [16384, 1024], P(('dp', 'tensor')), may hold values from -6 to 6
- lengths: int32 [16], P('dp'), may hold values from 256 to 1024, as said below
- query_weight: bfloat16 [1024, 1024], P(None, 'tensor'), may hold values from -0.1875 to 0.1875
- key_weight: bfloat16 [1024, 1024], P(None, 'tensor'), may hold values from -0.1875 to 0.1875
- value_weight: bfloat16 [1024, 1024], P(None, 'tensor'), may hold values from -0.1875 to 0.1875
- query_bias: float32 [1024], P('tensor'), may hold values from -3 to 3
- value_bias: float32 [1024], P('tensor'), may hold values from -3 to 3
- out_weight: bfloat16 [1024, 1024], P('tensor'), may hold values from -1 to 1
- out_bias: float32 [1024], replicated, may hold values from -3 to 3
- norm1_gain: float32 [1024], replicated, may hold values from 0.5 to 1.5
- norm1_bias: float32 [1024], replicated, may hold values from -2 to 2
- up_weight: bfloat16 [1024, 4096], P(None, 'tensor'), may hold values from -0.1875 to 0.1875
- up_bias: float32 [4096], P('tensor'), may hold values from -3 to 3
- down_weight: bfloat16 [4096, 1024], P('tensor'), may hold values from -0.09375 to 0.09375
- down_bias: float32 [1024], replicated, may hold values from -3 to 3
- norm2_gain: float32 [1024], replicated, may hold values from 0.5 to 1.5
- norm2_bias: float32 [1024], replicated, may hold values from -2 to 2
Outputs:
- outputs: bfloat16 [16384, 1024], P(('dp', 'tensor'))
- input_grad: float32 [16384, 1024], P(('dp', 'tensor'))
- query_weight_grad: float32 [1024, 1024], P(None, 'tensor')
- key_weight_grad: float32 [1024, 1024], P(None, 'tensor')
- value_weight_grad: float32 [1024, 1024], P(None, 'tensor')
- query_bias_grad: float32 [1024], P('tensor')
- value_bias_grad: float32 [1024], P('tensor')
- out_weight_grad: float32 [1024, 1024], P('tensor')
- out_bias_grad: float32 [1024], replicated
- norm1_gain_grad: float32 [1024], replicated
- norm1_bias_grad: float32 [1024], replicated
- up_weight_grad: float32 [1024, 4096], P(None, 'tensor')
- up_bias_grad: float32 [4096], P('tensor')
- down_weight_grad: float32 [4096, 1024], P('tensor')
- down_bias_grad: float32 [1024], replicated
- norm2_gain_grad: float32 [1024], replicated
- norm2_bias_grad: float32 [1024], replicated
Inputs may be any that keep to these rules, and one draw needn't show every extreme that they name: `lengths`: among the 2 sequences of each index of dp one has length 1024.
All inputs are finite; a program needn't handle non-finite values.
Results may differ from a plain program's by a relative error of at most 0.023.
Values may be sent and summed in bfloat16 or wider, within the bound.
A program may use at most 128 MiB of HBM per device.

v0:
```python
import functools

import jax
import jax.numpy as jnp
from jax import lax
from jax.experimental import pallas as pl
from jax.experimental.pallas import tpu as pltpu
from jax.sharding import PartitionSpec as P

HD = 64
LEN = 1024
PAIR = 2 * HD
GROUP = 8
F32 = jnp.float32
BF = jnp.bfloat16
NN = (((1,), (0,)), ((), ()))
NT = (((1,), (1,)), ((), ()))
TN = (((0,), (0,)), ((), ()))
MESH = pl.DeviceIdType.MESH
VMEM_LIMIT = 63 << 20


def product(left, right, dims=NN):
    return lax.dot_general(left, right, dims, preferred_element_type=F32)


def flip(index, bit):
    return index + bit * (1 - 2 * lax.rem(lax.div(index, bit), 2))


def mix(index, step):
    low = lax.rem(index + step, 2)
    high = lax.rem(lax.div(index, 2) + lax.div(step, 2), 2)
    return 2 * high + low


class Place:
    def __init__(self):
        self.dp = lax.axis_index("dp")
        self.t = lax.axis_index("tensor")
        self.e = lax.rem(self.dp, GROUP)
        self.core = lax.rem(self.e, 2)
        self.quad = lax.div(self.e, 2)
        self.to_core = (flip(self.dp, 1), self.t)
        self.to_x = (flip(self.dp, 2), self.t)
        self.to_y = (flip(self.dp, 4), self.t)
        self.quad_x = flip(self.quad, 1)
        self.quad_y = flip(self.quad, 2)
        self.quad_xy = flip(self.quad_x, 2)

    def to_z(self, step):
        return (self.dp, mix(self.t, jnp.int32(step)))

    def greet(self):
        barrier = pltpu.get_barrier_semaphore()
        peers = [self.to_core, self.to_x, self.to_y, self.to_z(1), self.to_z(2), self.to_z(3)]
        for peer in peers:
            pl.semaphore_signal(barrier, inc=1, device_id=peer, device_id_type=MESH)
        pl.semaphore_wait(barrier, len(peers))


def remote(src, dst, send, recv, index, device):
    return pltpu.make_async_remote_copy(
        src_ref=src,
        dst_ref=dst,
        send_sem=send.at[index],
        recv_sem=recv.at[index],
        device_id=device,
        device_id_type=MESH,
    )


class Spread:
    def __init__(self, place, full, sems, index):
        self.p = place
        self.full = full
        self.sems = sems
        self.index = index

    def block(self, step):
        return mix(self.p.t, jnp.int32(step)) if step else self.p.t

    def slot(self, step):
        return self.index * 4 + step

    def x_copy(self, step, src=None):
        p = self.p
        ref = self.full.at[self.block(step), p.quad, p.core]
        return remote(ref if src is None else src, ref, self.sems[0], self.sems[1], self.slot(step), p.to_x)

    def y_copy(self, step, src=None):
        p = self.p
        ref = self.full.at[self.block(step), p.quad, p.core]
        return remote(ref if src is None else src, ref, self.sems[2], self.sems[3], self.slot(step), p.to_y)

    def half_copies(self, step):
        p = self.p
        half = self.full.shape[3] // 2
        first = self.full.at[self.block(step), p.quad_x, p.core, pl.ds(0, half)]
        second = self.full.at[self.block(step), p.quad_y, p.core, pl.ds(half, half)]
        return (
            remote(first, first, self.sems[4], self.sems[5], self.slot(step), p.to_y),
            remote(second, second, self.sems[6], self.sems[7], self.slot(step), p.to_x),
        )

    def core_copy(self, step):
        p = self.p
        ref = self.full.at[self.block(step), :, p.core]
        return remote(ref, ref, self.sems[8], self.sems[9], self.slot(step), p.to_core)

    def first(self, step, src=None):
        self.x_copy(step, src).start()
        self.y_copy(step, src).start()

    def second(self, step):
        self.x_copy(step).wait_recv()
        self.y_copy(step).wait_recv()
        for copy in self.half_copies(step):
            copy.start()

    def third(self, step):
        for copy in self.half_copies(step):
            copy.wait_recv()
        self.core_copy(step).start()

    def arrived(self, step):
        self.core_copy(step).wait_recv()

    def finish(self, step):
        self.x_copy(step).wait_send()
        self.y_copy(step).wait_send()
        for copy in self.half_copies(step):
            copy.wait_send()
        self.core_copy(step).wait_send()

    @staticmethod
    def scratch(count):
        return [pltpu.SemaphoreType.DMA((4 * count,))] * 10


def norm_center(values):
    center = values - jnp.mean(values, axis=-1, keepdims=True)
    inverse = lax.rsqrt(jnp.mean(center * center, axis=-1, keepdims=True) + 1e-05)
    return center * inverse, inverse


def norm_back(grad, normal, inverse, gain):
    scaled = grad * gain
    first_mean = jnp.mean(scaled, axis=-1, keepdims=True)
    second_mean = jnp.mean(scaled * normal, axis=-1, keepdims=True)
    return inverse * (scaled - first_mean - normal * second_mean)


class Reduce:
    def __init__(self, place, bufs, sems):
        self.p = place
        self.g, self.s, self.rc, self.ra, self.rb, self.zs, self.rz, self.own = bufs
        self.sems = sems

    @staticmethod
    def scratch(piece, cols, arrays):
        return [
            pltpu.VMEM((2, 4, 2, piece, cols), BF),
            pltpu.VMEM((3, 4, piece, cols), BF),
            pltpu.VMEM((2, 4, piece, cols), BF),
            pltpu.VMEM((3, 2, piece // 2, cols), BF),
            pltpu.VMEM((3, 2, piece, cols), BF),
            pltpu.VMEM((3, piece, cols), BF),
            pltpu.VMEM((arrays, 3, piece, cols), BF),
            pltpu.VMEM((arrays, piece, cols), BF),
        ]

    @staticmethod
    def semaphores(units):
        return [pltpu.SemaphoreType.DMA((units,))] * 12

    def core_copy(self, u):
        other = 1 - self.p.core
        return remote(
            self.g.at[lax.rem(u, 2), :, other],
            self.rc.at[lax.rem(u, 2)],
            self.sems[0],
            self.sems[1],
            u,
            self.p.to_core,
        )

    def corner_copies(self, u):
        p, slot = self.p, lax.rem(u, 3)
        half = self.ra.shape[2]
        return (
            remote(
                self.s.at[slot, p.quad_xy, pl.ds(0, half)],
                self.ra.at[slot, 0],
                self.sems[2],
                self.sems[3],
                u,
                p.to_y,
            ),
            remote(
                self.s.at[slot, p.quad_xy, pl.ds(half, half)],
                self.ra.at[slot, 1],
                self.sems[4],
                self.sems[5],
                u,
                p.to_x,
            ),
        )

    def side_copies(self, u):
        p, slot = self.p, lax.rem(u, 3)
        return (
            remote(
                self.s.at[slot, p.quad_x], self.rb.at[slot, 0], self.sems[6], self.sems[7], u, p.to_x
            ),
            remote(
                self.s.at[slot, p.quad_y], self.rb.at[slot, 1], self.sems[8], self.sems[9], u, p.to_y
            ),
        )

    def z_copy(self, u, array, step):
        return remote(
            self.zs.at[lax.rem(u, 3)],
            self.rz.at[array, step - 1],
            self.sems[10],
            self.sems[11],
            array * 4 + step,
            (self.p.dp, mix(self.p.t, step)),
        )

    def free_g(self, u):
        if not isinstance(u, int):
            pl.when(u >= 2)(lambda: self.core_copy(u - 2).wait_send())
        elif u >= 2:
            self.core_copy(jnp.int32(u - 2)).wait_send()

    def send(self, u):
        self.core_copy(u).start()

    def fold_core(self, u):
        slot = lax.rem(u, 3)

        def freed():
            for copy in self.side_copies(u - 3) + self.corner_copies(u - 3):
                copy.wait_send()

        pl.when(u >= 3)(freed)
        self.core_copy(u).wait_recv()
        mine = self.g[lax.rem(u, 2), :, self.p.core].astype(F32)
        self.s[slot] = (mine + self.rc[lax.rem(u, 2)].astype(F32)).astype(BF)
        for copy in self.corner_copies(u):
            copy.start()

    def fold_corner(self, u):
        p, slot = self.p, lax.rem(u, 3)
        half = self.ra.shape[2]
        for copy in self.corner_copies(u):
            copy.wait_recv()
        lower = self.s[slot, p.quad_x, :half].astype(F32) + self.ra[slot, 0].astype(F32)
        self.s[slot, p.quad_x, :half] = lower.astype(BF)
        upper = self.s[slot, p.quad_y, half:].astype(F32) + self.ra[slot, 1].astype(F32)
        self.s[slot, p.quad_y, half:] = upper.astype(BF)
        for copy in self.side_copies(u):
            copy.start()

    def fold_sides(self, u, array, step, before):
        p, slot = self.p, lax.rem(u, 3)
        for copy in self.side_copies(u):
            copy.wait_recv()
        total = (
            self.s[slot, p.quad].astype(F32)
            + self.rb[slot, 0].astype(F32)
            + self.rb[slot, 1].astype(F32)
        ).astype(BF)

        if before is not None:
            old_array, old_step, valid = before
            pl.when(valid)(lambda: self.z_copy(u - 3, old_array, old_step).wait_send())

        def store():
            self.own[array] = total

        def pass_on():
            self.zs[slot] = total
            self.z_copy(u, array, step).start()

        pl.when(step == 0)(store)
        pl.when(step != 0)(pass_on)

    def finish(self, array):
        total = self.own[array].astype(F32)
        for step in (1, 2, 3):
            self.z_copy(jnp.int32(0), jnp.int32(array), jnp.int32(step)).wait_recv()
            total = total + self.rz[array, step - 1].astype(F32)
        self.own[array] = total.astype(BF)


def layer_kernel(
    len_ref,
    x_hbm,
    cot_hbm,
    vec_ref,
    bias_ref,
    wq_hbm,
    wk_hbm,
    wv_hbm,
    wo_hbm,
    wu_hbm,
    wd_hbm,
    qkv_full,
    out_full,
    up_full,
    down_full,
    q_hbm,
    k_hbm,
    v_hbm,
    outputs_hbm,
    down_grad,
    up_grad,
    proj_grad,
    acc,
    sums_ref,
    x_seq,
    bias_all,
    w_s,
    w_out,
    q_s,
    k_s,
    v_s,
    o_s,
    act_s,
    slope_s,
    wide,
    hidden_s,
    low_s,
    inverse_s,
    lse_s,
    d_att,
    kv_temp,
    rows_recv,
    small,
    small_recv,
    z_send,
    z_recv,
    bias_send,
    bias_recv,
    local,
    load,
    save,
    att_load,
    back_load,
    rows_send_sem,
    rows_recv_sem,
    small_ssem,
    small_rsem,
    *rest,
):
    p = Place()
    reduce = Reduce(p, rest[:8], rest[8:20])
    rows, model = acc.shape
    width = q_s.shape[2]
    half_index = lax.rem(p.t, 2)
    seq = lax.div(p.t, 2)
    own_at = pl.multiple_of(half_index * rows, rows)
    other_at = pl.multiple_of((1 - half_index) * rows, rows)
    own_rows, other_rows = pl.ds(own_at, rows), pl.ds(other_at, rows)
    fulls = [qkv_full, out_full, up_full, down_full]
    spreads = [Spread(p, full, rest[20:30], i) for i, full in enumerate(fulls)]
    QKV, OUT, UP, DOWN = range(4)
    qkv_cols = pl.ds(0, 3 * width)

    def on(step, at, *actions):
        @pl.when(step == at)
        def _():
            for action in actions:
                action()

    def begin(copies):
        for copy in copies:
            copy.start()

    def end(copies):
        for copy in copies:
            copy.wait()

    x_load = pltpu.make_async_copy(
        x_hbm.at[pl.ds(pl.multiple_of(seq * LEN, LEN), LEN)], x_seq, local.at[0]
    )
    own_loads = [
        pltpu.make_async_copy(w, w_s.at[2, :, :, :, pl.ds(i * width, width)], local.at[1 + i])
        for i, w in enumerate((wq_hbm, wk_hbm, wv_hbm))
    ]
    out_load = pltpu.make_async_copy(wo_hbm, w_out.at[0], local.at[4])
    up_load = pltpu.make_async_copy(wu_hbm, w_s.at[0], local.at[5])
    down_load = pltpu.make_async_copy(wd_hbm, w_s.at[0], local.at[6])
    cot_load = pltpu.make_async_copy(cot_hbm, low_s, local.at[7])
    qkv_save = pltpu.make_async_copy(w_s.at[2, :, :, :, qkv_cols], qkv_full.at[p.t], local.at[8])
    up_save = pltpu.make_async_copy(w_s.at[0], up_full.at[p.t], local.at[9])
    outputs_s = reduce.g.at[1, 0:2]
    outputs_save = pltpu.make_async_copy(outputs_s, outputs_hbm, local.at[10])
    begin(own_loads)
    x_load.start()
    out_load.start()
    up_load.start()
    cot_load.start()
    bias_all[p.t] = bias_ref[...]
    p.greet()

    def z_copies(array, step):
        slot = array * 4 + step
        if array == QKV:
            return [
                remote(
                    w.at[p.quad, p.core],
                    qkv_full.at[p.t, p.quad, p.core, :, pl.ds(i * width, width)],
                    z_send,
                    z_recv,
                    slot if i == 0 else 16 + 4 * (i - 1) + step,
                    p.to_z(step),
                )
                for i, w in enumerate((wq_hbm, wk_hbm, wv_hbm))
            ]
        w = (None, wo_hbm, wu_hbm, wd_hbm)[array]
        place = fulls[array].at[p.t, p.quad, p.core]
        return [remote(w.at[p.quad, p.core], place, z_send, z_recv, slot, p.to_z(step))]

    def bias_copy(step):
        return remote(bias_ref, bias_all.at[p.t], bias_send, bias_recv, step, p.to_z(step))

    for step in (1, 2, 3):
        bias_copy(step).start()
    for array in (QKV, OUT, UP, DOWN):
        for step in (1, 2, 3):
            begin(z_copies(array, step))

    def load_copy(array, step):
        if array == QKV:
            dst = w_s.at[2 + step % 2, :, :, :, qkv_cols]
        elif array == OUT:
            dst = w_out.at[step]
        else:
            dst = w_s.at[step]
        src = fulls[array].at[mix(p.t, jnp.int32(step))]
        return pltpu.make_async_copy(src, dst, load.at[array * 4 + step])

    def relay(plan):
        for array, legs in plan:
            spread = spreads[array]
            for leg in legs.split():
                kind, step = leg[0], int(leg[1])
                if kind == "f":
                    for copy in z_copies(array, step):
                        copy.wait_recv()
                    spread.first(step)
                elif kind == "s":
                    spread.second(step)
                elif kind == "t":
                    spread.third(step)
                else:
                    spread.arrived(step)
                    load_copy(array, step).start()

    def passed(step, place):
        plans = {
            (0, "end"): [
                (QKV, "f1 f2 s1 f3 s2"),
                (OUT, "f1"),
                (QKV, "t1"),
                (OUT, "f2 f3"),
                (QKV, "a1 s3"),
            ],
            (1, "mid"): [(QKV, "t2"), (OUT, "s1")],
            (1, "end"): [(OUT, "s2 s3"), (UP, "f1"), (QKV, "a2")],
            (2, "start"): [(QKV, "t3"), (OUT, "t1 t2")],
            (2, "mid"): [(OUT, "t3")],
            (2, "end"): [(QKV, "a3"), (OUT, "a1 a2 a3"), (UP, "f2")],
            (3, "start"): [(UP, "s1 f3")],
            (3, "end"): [(UP, "s2")],
        }
        for (at, where), plan in plans.items():
            if where == place:
                on(step, at, lambda plan=plan: relay(plan))

    def attend_saves(step):
        group, slot = mix(p.t, step), lax.rem(step, 2)
        pairs = ((q_s, q_hbm), (k_s, k_hbm), (v_s, v_hbm))
        return [
            pltpu.make_async_copy(vmem.at[slot], hbm.at[group], save.at[3 * step + i])
            for i, (vmem, hbm) in enumerate(pairs)
        ]

    def attend(step):
        group, slot = mix(p.t, step), lax.rem(step, 2)
        weights = w_s[2 + slot, :, :, :, qkv_cols].reshape(model, 3 * width)
        bias = bias_all[group, 0:1]
        queries = (product(x_seq[own_rows, :], weights[:, :width]) + bias[:, :width]).astype(BF)
        q_s[slot] = (queries.astype(F32) * HD ** (-0.5)).astype(BF)
        k_s[slot] = product(x_seq[...], weights[:, width : 2 * width]).astype(BF)
        v_s[slot] = (
            product(x_seq[...], weights[:, 2 * width :]) + bias[:, width : 2 * width]
        ).astype(BF)
        passed(step, "start")
        length = len_ref[seq]
        key_slot = lax.broadcasted_iota(jnp.int32, (LEN, rows), 0)
        lane = lax.broadcasted_iota(jnp.int32, (rows, PAIR), 1)
        for pair in range(width // PAIR):
            if pair == 1:
                passed(step, "mid")
            cols = slice(pair * PAIR, (pair + 1) * PAIR)
            keys, values, q_pair = k_s[slot, :, cols], v_s[slot, :, cols], q_s[slot, :, cols]
            parts = []
            for head in range(2):
                mine = jnp.where((lane >= HD) == (head == 1), q_pair, jnp.zeros_like(q_pair))
                scores = jnp.where(key_slot < length, product(keys, mine, NT), -1e30)
                top = jnp.max(scores, axis=0, keepdims=True)
                exponent = jnp.exp(scores - top)
                total = jnp.sum(exponent, axis=0, keepdims=True)
                mixed = product(values, exponent.astype(BF), TN)
                parts.append(mixed[head * HD : (head + 1) * HD] * (1.0 / total))
                lse_s[group, pl.ds(pair * 2 + head, 1), :] = top + jnp.log(total)
            o_s[step, :, cols] = jnp.concatenate(parts, axis=0).T.astype(BF)

    x_load.wait()
    end(own_loads)
    qkv_save.start()
    for step in (1, 2, 3):
        bias_copy(step).wait_recv()

    def attend_step(step, carry):
        for i in (1, 2, 3):
            on(step, i, load_copy(QKV, i).wait)
        pl.when(step >= 2)(lambda: end(attend_saves(step - 2)))
        attend(step)
        begin(attend_saves(step))
        on(step, 1, qkv_save.wait)
        passed(step, "end")
        return carry

    lax.fori_loop(0, 4, attend_step, 0)

    out_load.wait()
    for step in (1, 2, 3):
        load_copy(OUT, step).wait()
    acc[...] = x_seq[own_rows, :].astype(F32) + vec_ref[0:1]
    for step in range(4):
        acc[...] += product(o_s[step], w_out[step].reshape(width, model))
    normal1, inverse1 = norm_center(acc[...])
    wide[...] = normal1
    inverse_s[...] = jnp.broadcast_to(inverse1, inverse_s.shape)
    normed1 = normal1 * vec_ref[1:2] + vec_ref[2:3]
    hidden_s[...] = normed1.astype(BF)
    acc[...] = normed1 + vec_ref[3:4]
    relay([(UP, "t1")])

    def up_step(step, carry):
        on(step, 0, up_load.wait, up_save.start)
        for i in (1, 2, 3):
            on(step, i, load_copy(UP, i).wait)
        upper = product(hidden_s[...], w_s[step].reshape(model, model))
        upper = upper + bias_all[mix(p.t, step), 1:2]
        cdf = 0.5 * (1.0 + lax.erf(upper * 0.7071067811865476))
        act_s[step] = (upper * cdf).astype(BF)
        density = jnp.exp(-0.5 * upper * upper) * 0.3989422804014327
        slope_s[step] = (cdf + upper * density).astype(BF)
        on(step, 0, lambda: relay([(UP, "a1 s3"), (DOWN, "f1")]))
        on(step, 1, up_save.wait, down_load.start)
        on(step, 1, lambda: relay([(UP, "t2"), (DOWN, "f2"), (UP, "t3"), (DOWN, "f3"), (UP, "a2")]))
        on(step, 2, lambda: relay([(UP, "a3"), (DOWN, "s1")]))
        on(step, 3, lambda: relay([(DOWN, "s2")]))
        return carry

    lax.fori_loop(0, 4, up_step, 0)
    for step in (2, 3):
        end(attend_saves(jnp.int32(step)))

    def down_step(step, carry):
        on(step, 0, down_load.wait)
        for i in (1, 2, 3):
            on(step, i, load_copy(DOWN, i).wait)
        acc[...] += product(act_s[step], w_s[step].reshape(model, model))
        on(step, 0, lambda: relay([(DOWN, "s3 t1 t2 a1")]))
        on(step, 1, lambda: relay([(DOWN, "t3 a2")]))
        on(step, 2, lambda: relay([(DOWN, "a3")]))
        return carry

    lax.fori_loop(0, 4, down_step, 0)

    cot_load.wait()
    normal2, inverse2 = norm_center(acc[...])
    outputs = (normal2 * vec_ref[4:5] + vec_ref[5:6]).astype(BF)
    reduce.g[1, 0:2] = outputs.reshape(2, 2, rows // 4, model)
    outputs_save.start()
    slot_index = half_index * rows + lax.broadcasted_iota(jnp.int32, (rows, 1), 0)
    grad_out = jnp.where(slot_index < len_ref[seq], low_s[...].astype(F32), 0.0)
    d_second = norm_back(grad_out, normal2, inverse2, vec_ref[4:5])
    acc[...] = d_second
    low_s[...] = d_second.astype(BF)
    small[0] = jnp.zeros(small.shape[1:], F32)
    small[0, 0:1] = jnp.sum(grad_out * normal2, axis=0, keepdims=True)
    small[0, 1:2] = jnp.sum(grad_out, axis=0, keepdims=True)
    small[0, 2:3] = jnp.sum(d_second, axis=0, keepdims=True)

    grads = (down_grad, up_grad, proj_grad)
    back_spreads = [Spread(p, grad, rest[30:40], i) for i, grad in enumerate(grads)]
    for spread in back_spreads:
        spread.block = lambda step: 0
    B_DOWN, B_UP, B_PROJ = range(3)

    def group_at(i):
        return mix(p.t, 3 - i)

    def att_loads(i):
        g, slot = group_at(i), lax.rem(i, 2)
        pairs = ((q_hbm, q_s), (k_hbm, k_s), (v_hbm, v_s))
        return [
            pltpu.make_async_copy(hbm.at[g], vmem.at[slot], att_load.at[4 * i + n])
            for n, (hbm, vmem) in enumerate(pairs)
        ]

    def proj_load(i):
        slot = lax.rem(i, 2)
        return pltpu.make_async_copy(
            qkv_full.at[group_at(i)], w_s.at[slot, :, :, :, qkv_cols], att_load.at[4 * i + 3]
        )

    def up_again(step):
        return pltpu.make_async_copy(up_full.at[mix(p.t, step)], w_s.at[step], back_load.at[step])

    begin(att_loads(jnp.int32(0)))

    def mlp_order(i):
        return 3 - 2 * lax.rem(i, 2) - lax.div(i, 2)

    def unit_of(u):
        if isinstance(u, int) and u >= 8:
            return jnp.int32(B_PROJ), jnp.int32(11 - u)
        u = jnp.int32(u)
        return lax.rem(u, 2), mlp_order(lax.div(u, 2))

    def fold_core(u):
        reduce.fold_core(jnp.int32(u))

    def fold_corner(u):
        reduce.fold_corner(jnp.int32(u))

    def fold_sides(u):
        array, step = unit_of(u)
        if isinstance(u, int):
            old_array, old_step = unit_of(max(u - 3, 0))
            valid = jnp.logical_and(u >= 3, old_step != 0)
            u = jnp.int32(u)
        else:
            old_array, old_step = unit_of(jnp.maximum(u - 3, 0))
            valid = jnp.logical_and(u >= 3, old_step != 0)
        reduce.fold_sides(u, array, step, (old_array, old_step, valid))

    def tick(u):
        pl.when(u >= 4)(lambda: fold_sides(u - 4))
        pl.when(u >= 1)(lambda: fold_core(u - 1))
        reduce.send(u)
        pl.when(u >= 2)(lambda: fold_corner(u - 2))

    def store_unit(slot, left, right):
        part = model // 4
        for quad in range(4):
            terms = product(left(slice(quad * part, (quad + 1) * part)), right, TN)
            reduce.g[slot, quad] = terms.astype(BF).reshape(2, part // 2, right.shape[1])

    def mlp_step(i, carry):
        step = mlp_order(i)
        u = 2 * i
        reduce.free_g(u)
        store_unit(0, lambda cols: act_s[step, :, cols], low_s[...])
        tick(u)
        d_act = product(low_s[...], w_s[step].reshape(model, model), NT)
        d_up = (d_act * slope_s[step].astype(F32)).astype(BF)
        slope_s[step] = d_up
        up_again(step).start()
        at = pl.ds(6 + mix(p.t, step), 1)
        small[0, at, :] = jnp.sum(d_up.astype(F32), axis=0, keepdims=True)
        reduce.free_g(u + 1)
        on(i, 0, outputs_save.wait)
        store_unit(1, lambda cols: hidden_s[:, cols], slope_s[step])
        tick(u + 1)
        up_again(step).wait()
        acc[...] += product(slope_s[step], w_s[step].reshape(model, model), NT)
        return carry

    lax.fori_loop(0, 4, mlp_step, 0)

    proj_load(jnp.int32(0)).start()
    normal1 = wide[...]
    small[0, 3:4] = jnp.sum(acc[...] * normal1, axis=0, keepdims=True)
    small[0, 4:5] = jnp.sum(acc[...], axis=0, keepdims=True)
    d_first = norm_back(acc[...], normal1, inverse_s[:, 0:1], vec_ref[1:2])
    acc[...] = d_first
    low_s[...] = d_first.astype(BF)
    small[0, 5:6] = jnp.sum(d_first, axis=0, keepdims=True)
    d_own, d_other = act_s.at[0], act_s.at[1]

    def attend_back(i):
        slot = lax.rem(i, 2)
        g = group_at(i)
        step = mix(p.t, g)
        length = len_ref[seq]
        d_att[...] = product(low_s[...], w_out[step].reshape(width, model), NT).astype(BF)
        key_slot = lax.broadcasted_iota(jnp.int32, (LEN, rows), 0)
        lane = lax.broadcasted_iota(jnp.int32, (rows, PAIR), 1)
        for pair in range(width // PAIR):
            cols = slice(pair * PAIR, (pair + 1) * PAIR)
            keys, values, queries = k_s[slot, :, cols], v_s[slot, :, cols], q_s[slot, :, cols]
            d_out = d_att[:, cols]
            inner_all = (d_out.astype(F32) * o_s[step, :, cols].astype(F32)).T
            query_parts = []
            for head in range(2):
                mine = (lane >= HD) == (head == 1)
                own_q = jnp.where(mine, queries, jnp.zeros_like(queries))
                own_d = jnp.where(mine, d_out, jnp.zeros_like(d_out))
                inner = jnp.sum(inner_all[head * HD : (head + 1) * HD], axis=0, keepdims=True)
                scores = jnp.where(key_slot < length, product(keys, own_q, NT), -1e30)
                probs = jnp.exp(scores - lse_s[g, pl.ds(pair * 2 + head, 1), :])
                d_probs = product(values, own_d, NT)
                d_scores = (probs * (d_probs - inner) * HD ** (-0.5)).astype(BF)
                d_values = product(probs.astype(BF), own_d)
                d_keys = product(d_scores, own_q) * HD**0.5
                if head == 0:
                    kv_temp[0] = d_keys
                    kv_temp[1] = d_values
                else:
                    kv_temp[0] += d_keys
                    kv_temp[1] += d_values
                query_parts.append(product(keys, d_scores, TN)[head * HD : (head + 1) * HD])
            d_own[:, cols] = jnp.concatenate(query_parts, axis=0).T.astype(BF)
            for n in range(2):
                at = slice((n + 1) * width + pair * PAIR, (n + 1) * width + (pair + 1) * PAIR)
                d_own[:, at] = kv_temp[n, own_rows, :].astype(BF)
                d_other[:, at] = kv_temp[n, other_rows, :].astype(BF)

    def proj_unit(i, u):
        slot = lax.rem(i, 2)
        g = group_at(i)
        qkv, kv = slice(0, 3 * width), slice(width, 3 * width)
        at = pl.ds(10 + g, 1)
        small[0, at, qkv] = jnp.sum(d_own[:, qkv].astype(F32), axis=0, keepdims=True)
        small[0, at, kv] += jnp.sum(d_other[:, kv].astype(F32), axis=0, keepdims=True)
        reduce.core_copy(u - 2).wait_send()
        g_slot = lax.rem(u, 2)
        out_terms = product(o_s[mix(p.t, g)], low_s[...], TN).astype(BF)
        for quad in range(4):
            cols = slice(quad * width, (quad + 1) * width)
            block = (2, width // 2, width)
            x_own, x_other = x_seq[own_rows, cols], x_seq[other_rows, cols]
            queries = product(x_own, d_own[:, :width], TN)
            reduce.g[g_slot, quad, :, :, :width] = queries.astype(BF).reshape(block)
            both = product(x_own, d_own[:, kv], TN) + product(x_other, d_other[:, kv], TN)
            reduce.g[g_slot, quad, :, :, kv] = both.astype(BF).reshape(2, width // 2, 2 * width)
            reduce.g[g_slot, quad, :, :, 3 * width :] = out_terms[:, cols].reshape(block)
        reduce.send(u)
        proj_load(i).wait()
        weights = w_s[slot, :, :, :, qkv_cols].reshape(model, 3 * width)
        acc[...] += product(d_own[:, qkv], weights, NT)
        other = product(d_other[:, kv], weights[:, kv], NT)

        @pl.when(i == 0)
        def _():
            wide[...] = other

        @pl.when(i > 0)
        def _():
            wide[...] += other

    def own_save(array):
        place = grads[array].at[0, p.quad, p.core]
        return pltpu.make_async_copy(reduce.own.at[array], place, local.at[11 + array])

    def start_spread(array):
        reduce.finish(array)
        own_save(array).start()
        back_spreads[array].first(0, reduce.own.at[array])

    def end_spread(array):
        own_save(array).wait()
        back_spreads[array].third(0)

    def att_step(i, carry):
        end(att_loads(i))
        attend_back(i)

        def next_loads():
            begin(att_loads(i + 1))
            proj_load(i + 1).start()

        pl.when(i < 3)(next_loads)

        def passed_back(at):
            fold_sides(4 + at)
            fold_core(7 + at)
            fold_corner(6 + at)
            if at == 2:
                start_spread(B_DOWN)
            if at == 3:
                back_spreads[B_DOWN].second(0)
                start_spread(B_UP)

        for at in range(4):
            on(i, at, lambda at=at: passed_back(at))
        proj_unit(i, i + 8)
        return carry

    lax.fori_loop(0, 4, att_step, 0)
    rows_out = act_s.at[2]
    rows_out[...] = wide[...].astype(BF)
    rows_copy = remote(rows_out, rows_recv, rows_send_sem, rows_recv_sem, 0, p.to_z(1))
    rows_copy.start()
    peers = [p.to_core, p.to_x, p.to_y, p.to_z(1), p.to_z(2)]

    def small_copy(n):
        return remote(small.at[n], small_recv.at[n], small_ssem, small_rsem, n, peers[n])

    def small_next(n):
        small_copy(n).wait_recv()
        small[n + 1] = small[n] + small_recv[n]
        if n < 4:
            small_copy(n + 1).start()

    small_copy(0).start()
    fold_sides(8)
    fold_core(11)
    fold_corner(10)
    end_spread(B_DOWN)
    back_spreads[B_UP].second(0)
    small_next(0)
    fold_sides(9)
    fold_corner(11)
    end_spread(B_UP)
    small_next(1)
    fold_sides(10)
    small_next(2)
    fold_sides(11)
    start_spread(B_PROJ)
    small_next(3)
    back_spreads[B_PROJ].second(0)
    small_next(4)
    end_spread(B_PROJ)
    sums_ref[...] = small[5]

    for step in (1, 2, 3):
        bias_copy(step).wait_send()
        for array in range(4):
            for copy in z_copies(array, step):
                copy.wait_send()
            spreads[array].finish(step)
    rows_copy.wait_recv()
    acc[...] += rows_recv[...].astype(F32)
    rows_copy.wait_send()
    for u in (10, 11):
        reduce.core_copy(jnp.int32(u)).wait_send()
    for u in (9, 10, 11):
        for copy in reduce.side_copies(jnp.int32(u)) + reduce.corner_copies(jnp.int32(u)):
            copy.wait_send()
    for u in (9, 10):
        array, step = unit_of(u)
        reduce.z_copy(jnp.int32(u), array, step).wait_send()
    for n in range(5):
        small_copy(n).wait_send()
    for spread in back_spreads:
        spread.arrived(0)
        spread.finish(0)


def run_layer(lengths, x, cot, vec, bias, wq, wk, wv, wo, wu, wd):
    T = lax.axis_size("tensor")
    model = x.shape[1]
    rows = x.shape[0] // T
    width = wo.shape[0]
    piece = model // GROUP

    def pieces(w):
        return w.reshape(4, 2, w.shape[0] // GROUP, w.shape[1])

    def out(*shape, dtype=BF):
        return jax.ShapeDtypeStruct(shape, dtype)

    anyw = pl.BlockSpec(memory_space=pl.ANY)
    vmem = pl.BlockSpec(memory_space=pltpu.VMEM)
    smem = pl.BlockSpec(memory_space=pltpu.SMEM)
    dma = pltpu.SemaphoreType.DMA
    outs = [
        out(T, 4, 2, piece, 3 * width),
        out(T, 4, 2, width // GROUP, model),
        out(T, 4, 2, piece, model),
        out(T, 4, 2, piece, model),
        out(T, rows, width),
        out(T, LEN, width),
        out(T, LEN, width),
        out(2, 2, rows // 4, model),
        *[out(1, 4, 2, piece, model)] * 3,
        out(rows, model, dtype=F32),
        out(16, model, dtype=F32),
    ]
    return pl.pallas_call(
        layer_kernel,
        in_specs=[smem, anyw, anyw, vmem, vmem] + [anyw] * 6,
        out_specs=[anyw] * 11 + [vmem] * 2,
        out_shape=outs,
        scratch_shapes=[
            pltpu.VMEM((LEN, model), BF),
            pltpu.VMEM((T, 8, model), F32),
            pltpu.VMEM((4, 4, 2, piece, model), BF),
            pltpu.VMEM((T, 4, 2, width // GROUP, model), BF),
            pltpu.VMEM((2, rows, width), BF),
            pltpu.VMEM((2, LEN, width), BF),
            pltpu.VMEM((2, LEN, width), BF),
            pltpu.VMEM((T, rows, width), BF),
            pltpu.VMEM((T, rows, model), BF),
            pltpu.VMEM((T, rows, model), BF),
            pltpu.VMEM((rows, model), F32),
            pltpu.VMEM((rows, model), BF),
            pltpu.VMEM((rows, model), BF),
            pltpu.VMEM((rows, 128), F32),
            pltpu.VMEM((T, 8, rows), F32),
            pltpu.VMEM((rows, width), BF),
            pltpu.VMEM((2, LEN, PAIR), F32),
            pltpu.VMEM((rows, model), BF),
            pltpu.VMEM((6, 16, model), F32),
            pltpu.VMEM((5, 16, model), F32),
            dma((24,)),
            dma((24,)),
            dma((4,)),
            dma((4,)),
            dma((14,)),
            dma((16,)),
            dma((12,)),
            dma((16,)),
            dma((4,)),
            dma((1,)),
            dma((1,)),
            dma((5,)),
            dma((5,)),
            *Reduce.scratch(piece, model, 3),
            *Reduce.semaphores(12),
            *Spread.scratch(4),
            *Spread.scratch(3),
        ],
        compiler_params=pltpu.CompilerParams(
            collective_id=0, has_side_effects=True, vmem_limit_bytes=VMEM_LIMIT
        ),
        cost_estimate=pl.CostEstimate(
            flops=100 * 10**9, bytes_accessed=120 << 20, transcendentals=24 << 20
        ),
        name="layer",
    )(
        lengths,
        x,
        cot,
        vec,
        bias,
        pieces(wq),
        pieces(wk),
        pieces(wv),
        pieces(wo),
        pieces(wu),
        pieces(wd),
    )


def on_device(
    inputs,
    cotangent,
    lengths,
    query_weight,
    key_weight,
    value_weight,
    query_bias,
    value_bias,
    out_weight,
    out_bias,
    norm1_gain,
    norm1_bias,
    up_weight,
    up_bias,
    down_weight,
    down_bias,
    norm2_gain,
    norm2_bias,
):
    t = lax.axis_index("tensor")
    model = inputs.shape[1]
    rows = cotangent.shape[0]
    width = out_weight.shape[0]
    zero_row = jnp.zeros((model,), F32)
    vec = jnp.stack(
        [out_bias, norm1_gain, norm1_bias, down_bias, norm2_gain, norm2_bias, zero_row, zero_row]
    )
    bias = jnp.stack(
        [jnp.concatenate([query_bias, value_bias, zero_row[2 * width :]]), up_bias] + [zero_row] * 6
    )
    results = run_layer(
        lengths,
        inputs,
        cotangent,
        vec,
        bias,
        query_weight,
        key_weight,
        value_weight,
        out_weight,
        up_weight,
        down_weight,
    )
    outputs, down_grad, up_grad, proj_grad, input_grad, sums = results[7:]
    grads = [g.reshape(model, model).astype(F32) for g in (down_grad, up_grad, proj_grad)]
    size = lax.axis_size("dp")
    if size > GROUP:
        groups = [list(range(first, size, GROUP)) for first in range(GROUP)]
        *grads, sums = lax.psum((*grads, sums), "dp", axis_index_groups=groups)
    down_grad, up_grad, proj_grad = grads
    up_bias_grad = lax.dynamic_index_in_dim(sums[6:10], t, 0, keepdims=False)
    proj_bias = lax.dynamic_index_in_dim(sums[10:14], t, 0, keepdims=False)
    out_grad = jnp.concatenate(
        [proj_grad[c * width : (c + 1) * width, 3 * width :] for c in range(4)], axis=1
    )
    return (
        outputs.reshape(rows, model),
        input_grad,
        proj_grad[:, :width],
        proj_grad[:, width : 2 * width],
        proj_grad[:, 2 * width : 3 * width],
        proj_bias[:width],
        proj_bias[2 * width : 3 * width],
        out_grad,
        sums[5],
        sums[3],
        sums[4],
        up_grad,
        up_bias_grad,
        down_grad,
        sums[2],
        sums[0],
        sums[1],
    )


def solution(mesh):
    rows = P(("dp", "tensor"), None)
    by_col = P(None, "tensor")
    by_row = P("tensor", None)
    split = P("tensor")
    whole = P()
    return jax.shard_map(
        on_device,
        mesh=mesh,
        in_specs=(
            P("dp", None),
            rows,
            P("dp"),
            by_col,
            by_col,
            by_col,
            split,
            split,
            by_row,
            whole,
            whole,
            whole,
            by_col,
            split,
            by_row,
            whole,
            whole,
            whole,
        ),
        out_specs=(
            rows,
            rows,
            by_col,
            by_col,
            by_col,
            split,
            split,
            by_row,
            whole,
            whole,
            whole,
            by_col,
            split,
            by_row,
            whole,
            whole,
            whole,
        ),
        check_vma=False,
    )
```

profile of v0, /device:TPU:0, one launch (start us, length us, event | category | flops | bytes accessed | tf_op | source)
XLA Modules:
  0.0 294.3 jit_solution(12987780968593846393)
XLA Ops:
  0.7 0.7 pad_maximum_fusion.1
  1.4 0.1 pad.7.clone
  1.5 1.4 maximum_maximum_fusion.bias_ref
  2.8 1.4 stack.39.vec_ref
  4.3 272.2 %layer.1 = (bf16[4,4,2,128,768]{4,3,2,1,0:T(8,128)(2,1)}, bf16[4,4,2,32,1024]{4,3,2,1,0:T(8,128)(2,1)}, bf16[4,4,2,128,1024]{4,3,2,1,0:T(8,128)(2,1)}, bf16[4,4,...) custom-call(s32[2]{0:T(128)} %len_ref.1, ...), custom_call_target="tpu_custom_call" | custom-call | flops 99999997952 | bytes 125829120 | tf_op jit(solution)/shard_map/layer/pallas_call | solution.py:901
  276.4 2.0 bitcast_convert_fusion.2
  278.5 0.0 copy-start
  278.5 0.0 copy-start.5
  278.5 0.0 copy-start.3
  278.5 0.1 fusion
  278.6 1.1 pad_maximum_fusion
  279.7 1.3 copy-done
  281.0 0.0 copy-done.5
  281.0 0.6 fusion.4
  281.7 0.6 constant_dynamic-slice_fusion.1
  282.3 0.0 copy-done.3
  282.3 6.3 %bitcast_convert_fusion = (f32[1024,1024]{1,0:T(8,128)}, f32[1024,1024]{1,0:T(8,128)}) fusion(bf16[1,4,2,128,1024]{4,3,2,1,0:T(8,128)(2,1)S(1)} %copy-done.3, bf16[1,4,2,128,1024]{4,3,2,1,0:T(8,128)(2,1)} %get-tuple-element.27), kind=kLoop, calls=%fused_computation | loop fusion | flops 2097152 | bytes 12582912 | tf_op jit(solution)/shard_map/convert_element_type | solution.py:1012
  288.6 0.6 fusion.2
  289.2 0.0 copy-done.1
  289.2 1.8 fusion.1
  291.0 0.0 copy-done.4
  291.0 1.0 copy.37
  292.0 1.0 copy-done.2
  293.0 1.3 copy.38
  (7 shorter events, 0.0 us)
Async XLA Ops:
  278.5 2.5 copy-start
  278.5 2.5 copy-start.5
  278.5 3.8 %copy-start.3 = (bf16[1,4,2,128,1024]{4,3,2,1,0:T(8,128)(2,1)S(1)}, bf16[1,4,2,128,1024]{4,3,2,1,0:T(8,128)(2,1)}, u32[]{:S(2)}) copy-start(bf16[1,4,2,128,1024]{4,3,2,1,0:T(8,128)(2,1)} %get-tuple-element.28) | copy-start | bytes 6291460
  282.3 6.9 %copy-start.1 = (f32[1024,1024]{1,0:T(8,128)S(1)}, f32[1024,1024]{1,0:T(8,128)}, u32[]{:S(2)}) copy-start(f32[1024,1024]{1,0:T(8,128)} %copy-done) | copy-start | bytes 12582916
  289.2 1.8 copy-start.4
  291.0 2.0 copy-start.2
where the time goes:
time: 295 us; the launch traced here: 294 us
  Pallas kernels  272 us (92%)
  other arithmetic  11.5 us (4%)
  local copies, waits for them, and re-layouts  9.84 us (3%)
    pallas_call x1, Pallas kernels, run_layer(): pl.pallas_call(layer_kernel, in_specs=[smem, anyw, anyw, vmem, vmem] + [a...  272 us
    convert_element_type x2, other arithmetic, on_device(): g.reshape(model, model).astype(F32)  8.36 us

commit v1 on v0

--- a/solution.py
+++ b/solution.py
@@ -299,8 +299,15 @@
     len_ref,
     x_hbm,
     cot_hbm,
-    vec_ref,
-    bias_ref,
+    out_bias_ref,
+    gain1_ref,
+    shift1_ref,
+    down_bias_ref,
+    gain2_ref,
+    shift2_ref,
+    query_bias_ref,
+    value_bias_ref,
+    up_bias_ref,
     wq_hbm,
     wk_hbm,
     wv_hbm,
@@ -321,6 +328,7 @@
     acc,
     sums_ref,
     x_seq,
+    bias_s,
     bias_all,
     w_s,
     w_out,
@@ -403,7 +411,11 @@
     out_load.start()
     up_load.start()
     cot_load.start()
-    bias_all[p.t] = bias_ref[...]
+    bias_s[...] = jnp.zeros(bias_s.shape, F32)
+    bias_s[0:1, :width] = query_bias_ref[...]
+    bias_s[0:1, width : 2 * width] = value_bias_ref[...]
+    bias_s[1:2] = up_bias_ref[...]
+    bias_all[p.t] = bias_s[...]
     p.greet()
 
     def z_copies(array, step):
@@ -425,7 +437,7 @@
         return [remote(w.at[p.quad, p.core], place, z_send, z_recv, slot, p.to_z(step))]
 
     def bias_copy(step):
-        return remote(bias_ref, bias_all.at[p.t], bias_send, bias_recv, step, p.to_z(step))
+        return remote(bias_s, bias_all.at[p.t], bias_send, bias_recv, step, p.to_z(step))
 
     for step in (1, 2, 3):
         bias_copy(step).start()
@@ -541,15 +553,15 @@
     out_load.wait()
     for step in (1, 2, 3):
         load_copy(OUT, step).wait()
-    acc[...] = x_seq[own_rows, :].astype(F32) + vec_ref[0:1]
+    acc[...] = x_seq[own_rows, :].astype(F32) + out_bias_ref[...]
     for step in range(4):
         acc[...] += product(o_s[step], w_out[step].reshape(width, model))
     normal1, inverse1 = norm_center(acc[...])
     wide[...] = normal1
     inverse_s[...] = jnp.broadcast_to(inverse1, inverse_s.shape)
-    normed1 = normal1 * vec_ref[1:2] + vec_ref[2:3]
+    normed1 = normal1 * gain1_ref[...] + shift1_ref[...]
     hidden_s[...] = normed1.astype(BF)
-    acc[...] = normed1 + vec_ref[3:4]
+    acc[...] = normed1 + down_bias_ref[...]
     relay([(UP, "t1")])
 
     def up_step(step, carry):
@@ -587,12 +599,12 @@
 
     cot_load.wait()
     normal2, inverse2 = norm_center(acc[...])
-    outputs = (normal2 * vec_ref[4:5] + vec_ref[5:6]).astype(BF)
+    outputs = (normal2 * gain2_ref[...] + shift2_ref[...]).astype(BF)
     reduce.g[1, 0:2] = outputs.reshape(2, 2, rows // 4, model)
     outputs_save.start()
     slot_index = half_index * rows + lax.broadcasted_iota(jnp.int32, (rows, 1), 0)
     grad_out = jnp.where(slot_index < len_ref[seq], low_s[...].astype(F32), 0.0)
-    d_second = norm_back(grad_out, normal2, inverse2, vec_ref[4:5])
+    d_second = norm_back(grad_out, normal2, inverse2, gain2_ref[...])
     acc[...] = d_second
     low_s[...] = d_second.astype(BF)
     small[0] = jnp.zeros(small.shape[1:], F32)
@@ -692,7 +704,7 @@
     normal1 = wide[...]
     small[0, 3:4] = jnp.sum(acc[...] * normal1, axis=0, keepdims=True)
     small[0, 4:5] = jnp.sum(acc[...], axis=0, keepdims=True)
-    d_first = norm_back(acc[...], normal1, inverse_s[:, 0:1], vec_ref[1:2])
+    d_first = norm_back(acc[...], normal1, inverse_s[:, 0:1], gain1_ref[...])
     acc[...] = d_first
     low_s[...] = d_first.astype(BF)
     small[0, 5:6] = jnp.sum(d_first, axis=0, keepdims=True)
@@ -810,8 +822,15 @@
     lax.fori_loop(0, 4, att_step, 0)
     rows_out = act_s.at[2]
     rows_out[...] = wide[...].astype(BF)
-    rows_copy = remote(rows_out, rows_recv, rows_send_sem, rows_recv_sem, 0, p.to_z(1))
-    rows_copy.start()
+
+    def rows_copy(part):
+        at = pl.ds(part * (rows // 4), rows // 4)
+        return remote(
+            rows_out.at[at], rows_recv.at[at], rows_send_sem, rows_recv_sem, part, p.to_z(1)
+        )
+
+    rows_copy(0).start()
+    rows_copy(1).start()
     peers = [p.to_core, p.to_x, p.to_y, p.to_z(1), p.to_z(2)]
 
     def small_copy(n):
@@ -831,10 +850,12 @@
     back_spreads[B_UP].second(0)
     small_next(0)
     fold_sides(9)
+    rows_copy(2).start()
     fold_corner(11)
     end_spread(B_UP)
     small_next(1)
     fold_sides(10)
+    rows_copy(3).start()
     small_next(2)
     fold_sides(11)
     start_spread(B_PROJ)
@@ -850,9 +871,9 @@
             for copy in z_copies(array, step):
                 copy.wait_send()
             spreads[array].finish(step)
-    rows_copy.wait_recv()
+    for part in range(4):
+        rows_copy(part).wait()
     acc[...] += rows_recv[...].astype(F32)
-    rows_copy.wait_send()
     for u in (10, 11):
         reduce.core_copy(jnp.int32(u)).wait_send()
     for u in (9, 10, 11):
@@ -868,7 +889,7 @@
         spread.finish(0)
 
 
-def run_layer(lengths, x, cot, vec, bias, wq, wk, wv, wo, wu, wd):
+def run_layer(lengths, x, cot, vectors, wq, wk, wv, wo, wu, wd):
     T = lax.axis_size("tensor")
     model = x.shape[1]
     rows = x.shape[0] // T
@@ -900,11 +921,12 @@
     ]
     return pl.pallas_call(
         layer_kernel,
-        in_specs=[smem, anyw, anyw, vmem, vmem] + [anyw] * 6,
+        in_specs=[smem, anyw, anyw] + [vmem] * 9 + [anyw] * 6,
         out_specs=[anyw] * 11 + [vmem] * 2,
         out_shape=outs,
         scratch_shapes=[
             pltpu.VMEM((LEN, model), BF),
+            pltpu.VMEM((8, model), F32),
             pltpu.VMEM((T, 8, model), F32),
             pltpu.VMEM((4, 4, 2, piece, model), BF),
             pltpu.VMEM((T, 4, 2, width // GROUP, model), BF),
@@ -933,8 +955,8 @@
             dma((12,)),
             dma((16,)),
             dma((4,)),
-            dma((1,)),
-            dma((1,)),
+            dma((4,)),
+            dma((4,)),
             dma((5,)),
             dma((5,)),
             *Reduce.scratch(piece, model, 3),
@@ -953,8 +975,7 @@
         lengths,
         x,
         cot,
-        vec,
-        bias,
+        *[v.reshape(1, -1) for v in vectors],
         pieces(wq),
         pieces(wk),
         pieces(wv),
@@ -962,6 +983,78 @@
         pieces(wu),
         pieces(wd),
     )
+
+
+def results_kernel(
+    outputs_in,
+    down_in,
+    up_in,
+    proj_in,
+    input_in,
+    sums_in,
+    outputs_ref,
+    input_ref,
+    query_ref,
+    key_ref,
+    value_ref,
+    query_bias_ref,
+    value_bias_ref,
+    out_ref,
+    out_bias_ref,
+    gain1_ref,
+    shift1_ref,
+    up_ref,
+    up_bias_ref,
+    down_ref,
+    down_bias_ref,
+    gain2_ref,
+    shift2_ref,
+):
+    t = lax.axis_index("tensor")
+    width = query_ref.shape[1]
+    outputs_ref[...] = outputs_in[...]
+    input_ref[...] = input_in[...]
+    down_ref[...] = down_in[...].astype(F32)
+    up_ref[...] = up_in[...].astype(F32)
+    for n, ref in enumerate((query_ref, key_ref, value_ref, out_ref)):
+        ref[...] = proj_in[:, n * width : (n + 1) * width].astype(F32)
+    rows = (gain2_ref, shift2_ref, down_bias_ref, gain1_ref, shift1_ref, out_bias_ref)
+    for n, ref in enumerate(rows):
+        ref[...] = sums_in[n : n + 1]
+    up_bias_ref[...] = sums_in[pl.ds(6 + t, 1), :]
+    proj = sums_in[pl.ds(10 + t, 1), :]
+    query_bias_ref[...] = proj[:, :width]
+    value_bias_ref[...] = proj[:, 2 * width : 3 * width]
+
+
+def run_results(outputs, down, up, proj, input_grad, sums, width):
+    rows, model = outputs.shape
+    steps = 4
+    tall = lambda count, cols=model: pl.BlockSpec((count // steps, cols), lambda i: (i, 0))
+    row = lambda cols=model: pl.BlockSpec((1, cols), lambda i: (0, 0))
+    out = lambda count, cols=model, dtype=F32: jax.ShapeDtypeStruct((count, cols), dtype)
+    whole = pl.BlockSpec(sums.shape, lambda i: (0, 0))
+    outs = [
+        (out(rows, dtype=BF), tall(rows)),
+        (out(rows), tall(rows)),
+        *[(out(model, width), tall(model, width))] * 3,
+        *[(out(1, width), row(width))] * 2,
+        (out(width), pl.BlockSpec((width, model // steps), lambda i: (0, i))),
+        *[(out(1), row())] * 3,
+        (out(model), tall(model)),
+        (out(1), row()),
+        (out(model), tall(model)),
+        *[(out(1), row())] * 3,
+    ]
+    return pl.pallas_call(
+        results_kernel,
+        grid=(steps,),
+        in_specs=[tall(rows), tall(model), tall(model), tall(model), tall(rows), whole],
+        out_specs=[spec for _, spec in outs],
+        out_shape=[shape for shape, _ in outs],
+        compiler_params=pltpu.CompilerParams(vmem_limit_bytes=VMEM_LIMIT),
+        name="results",
+    )(outputs, down, up, proj, input_grad, sums)
 
 
 def on_device(
@@ -984,23 +1077,24 @@
     norm2_gain,
     norm2_bias,
 ):
-    t = lax.axis_index("tensor")
     model = inputs.shape[1]
     rows = cotangent.shape[0]
     width = out_weight.shape[0]
-    zero_row = jnp.zeros((model,), F32)
-    vec = jnp.stack(
-        [out_bias, norm1_gain, norm1_bias, down_bias, norm2_gain, norm2_bias, zero_row, zero_row]
-    )
-    bias = jnp.stack(
-        [jnp.concatenate([query_bias, value_bias, zero_row[2 * width :]]), up_bias] + [zero_row] * 6
-    )
     results = run_layer(
         lengths,
         inputs,
         cotangent,
-        vec,
-        bias,
+        (
+            out_bias,
+            norm1_gain,
+            norm1_bias,
+            down_bias,
+            norm2_gain,
+            norm2_bias,
+            query_bias,
+            value_bias,
+            up_bias,
+        ),
         query_weight,
         key_weight,
         value_weight,
@@ -1009,36 +1103,14 @@
         down_weight,
     )
     outputs, down_grad, up_grad, proj_grad, input_grad, sums = results[7:]
-    grads = [g.reshape(model, model).astype(F32) for g in (down_grad, up_grad, proj_grad)]
+    grads = [g.reshape(model, model) for g in (down_grad, up_grad, proj_grad)]
     size = lax.axis_size("dp")
     if size > GROUP:
+        grads = [g.astype(F32) for g in grads]
         groups = [list(range(first, size, GROUP)) for first in range(GROUP)]
         *grads, sums = lax.psum((*grads, sums), "dp", axis_index_groups=groups)
-    down_grad, up_grad, proj_grad = grads
-    up_bias_grad = lax.dynamic_index_in_dim(sums[6:10], t, 0, keepdims=False)
-    proj_bias = lax.dynamic_index_in_dim(sums[10:14], t, 0, keepdims=False)
-    out_grad = jnp.concatenate(
-        [proj_grad[c * width : (c + 1) * width, 3 * width :] for c in range(4)], axis=1
-    )
-    return (
-        outputs.reshape(rows, model),
-        input_grad,
-        proj_grad[:, :width],
-        proj_grad[:, width : 2 * width],
-        proj_grad[:, 2 * width : 3 * width],
-        proj_bias[:width],
-        proj_bias[2 * width : 3 * width],
-        out_grad,
-        sums[5],
-        sums[3],
-        sums[4],
-        up_grad,
-        up_bias_grad,
-        down_grad,
-        sums[2],
-        sums[0],
-        sums[1],
-    )
+    done = run_results(outputs.reshape(rows, model), *grads, input_grad, sums, width)
+    return tuple(v.reshape(-1) if v.shape[0] == 1 else v for v in done)
 
 
 def solution(mesh):

time: 295 us -> 279 us (0.946)
  other arithmetic: 11.5 us -> 0 us
  local copies, waits for them, and re-layouts: 9.84 us -> 0 us
  Pallas kernels: 272 us -> 278 us
    convert_element_type x2 -> x0, other arithmetic: 8.36 us -> none  [on_device(): g.reshape(model, model).astype(F32)]
    pallas_call x1 -> x2, Pallas kernels: 272 us -> 278 us  [the longest x1 267 us: run_layer(): pl.pallas_call(layer_kernel, in_specs=[smem, anyw, anyw] + [vmem] * 9 + [...]
    unnamed x14 -> x0, local copies, waits for them, and re-layouts: 4.58 us -> none
    slice x6 -> x0, local copies, waits for them, and re-layouts: 3.16 us -> none  [the longest x1 1.78 us: on_device(): proj_grad[:, 2 * width:3 * width]]
where the time goes in v1:
time: 279 us; the launch traced here: 278 us
  Pallas kernels  278 us (100%)
    pallas_call x1, Pallas kernels, run_layer(): pl.pallas_call(layer_kernel, in_specs=[smem, anyw, anyw] + [vmem] * 9 + [...  267 us
    pallas_call x1, Pallas kernels, run_results(): pl.pallas_call(results_kernel, grid=(steps,), in_specs=[tall(rows), tall(...  10.3 us

profile of v1, /device:TPU:0, one launch (start us, length us, event | category | flops | bytes accessed | tf_op | source)
XLA Modules:
  0.0 278.5 jit_solution(13887100625047979010)
XLA Ops:
  0.7 267.3 %layer.1 = (bf16[4,4,2,128,768]{4,3,2,1,0:T(8,128)(2,1)}, bf16[4,4,2,32,1024]{4,3,2,1,0:T(8,128)(2,1)}, bf16[4,4,2,128,1024]{4,3,2,1,0:T(8,128)(2,1)}, bf16[4,4,...) custom-call(s32[2]{0:T(128)} %len_ref.1, ...), custom_call_target="tpu_custom_call" | custom-call | flops 99999997952 | bytes 125829120 | tf_op jit(solution)/shard_map/layer/pallas_call | solution.py:922
  268.0 10.3 %results.1 = (bf16[512,1024]{1,0:T(8,128)(2,1)}, f32[512,1024]{1,0:T(8,128)}, f32[1024,256]{1,0:T(8,128)}, f32[1024,256]{1,0:T(8,128)}, f32[1024,256]{1,0:T(8,12...) custom-call(bf16[512,1024]{1,0:T(8,128)(2,1)} %bitcast.31, ...), custom_call_target="tpu_custom_call" | custom-call | tf_op jit(solution)/shard_map/results/pallas_call | solution.py:1049

commit v2 on v1

--- a/solution.py
+++ b/solution.py
@@ -71,7 +71,8 @@
 
 
 class Spread:
-    def __init__(self, place, full, sems, index):
+    def __init__(self, place, full, sems, index, doubled=()):
+        self.doubled = doubled
         self.p = place
         self.full = full
         self.sems = sems
@@ -86,18 +87,25 @@
     def x_copy(self, step, src=None):
         p = self.p
         ref = self.full.at[self.block(step), p.quad, p.core]
+        if step in self.doubled:
+            half = self.full.shape[3] // 2
+            ref = ref.at[pl.ds(0, half)]
         return remote(ref if src is None else src, ref, self.sems[0], self.sems[1], self.slot(step), p.to_x)
 
     def y_copy(self, step, src=None):
         p = self.p
         ref = self.full.at[self.block(step), p.quad, p.core]
+        if step in self.doubled:
+            half = self.full.shape[3] // 2
+            ref = ref.at[pl.ds(half, half)]
         return remote(ref if src is None else src, ref, self.sems[2], self.sems[3], self.slot(step), p.to_y)
 
     def half_copies(self, step):
         p = self.p
         half = self.full.shape[3] // 2
-        first = self.full.at[self.block(step), p.quad_x, p.core, pl.ds(0, half)]
-        second = self.full.at[self.block(step), p.quad_y, p.core, pl.ds(half, half)]
+        low, high = (half, 0) if step in self.doubled else (0, half)
+        first = self.full.at[self.block(step), p.quad_x, p.core, pl.ds(low, half)]
+        second = self.full.at[self.block(step), p.quad_y, p.core, pl.ds(high, half)]
         return (
             remote(first, first, self.sems[4], self.sems[5], self.slot(step), p.to_y),
             remote(second, second, self.sems[6], self.sems[7], self.slot(step), p.to_x),
@@ -111,6 +119,9 @@
     def first(self, step, src=None):
         self.x_copy(step, src).start()
         self.y_copy(step, src).start()
+        if step in self.doubled:
+            for copy in self.half_copies(step):
+                copy.start()
 
     def second(self, step):
         self.x_copy(step).wait_recv()
@@ -119,6 +130,9 @@
             copy.start()
 
     def third(self, step):
+        if step in self.doubled:
+            self.x_copy(step).wait_recv()
+            self.y_copy(step).wait_recv()
         for copy in self.half_copies(step):
             copy.wait_recv()
         self.core_copy(step).start()
@@ -373,8 +387,11 @@
     other_at = pl.multiple_of((1 - half_index) * rows, rows)
     own_rows, other_rows = pl.ds(own_at, rows), pl.ds(other_at, rows)
     fulls = [qkv_full, out_full, up_full, down_full]
-    spreads = [Spread(p, full, rest[20:30], i) for i, full in enumerate(fulls)]
     QKV, OUT, UP, DOWN = range(4)
+    spreads = [
+        Spread(p, full, rest[20:30], i, (1,) if i in (UP, DOWN) else ())
+        for i, full in enumerate(fulls)
+    ]
     qkv_cols = pl.ds(0, 3 * width)
 
     def on(step, at, *actions):
@@ -434,7 +451,16 @@
             ]
         w = (None, wo_hbm, wu_hbm, wd_hbm)[array]
         place = fulls[array].at[p.t, p.quad, p.core]
-        return [remote(w.at[p.quad, p.core], place, z_send, z_recv, slot, p.to_z(step))]
+        copies = [remote(w.at[p.quad, p.core], place, z_send, z_recv, slot, p.to_z(step))]
+        if step in spreads[array].doubled:
+            half = w.shape[2] // 2
+            for n, quad in enumerate((p.quad_y, p.quad_x)):
+                at = pl.ds(n * half, half)
+                src = w.at[quad, p.core, at]
+                dst = fulls[array].at[p.t, quad, p.core, at]
+                extra = 24 + 2 * (array - UP) + n
+                copies.append(remote(src, dst, z_send, z_recv, extra, p.to_z(step)))
+        return copies
 
     def bias_copy(step):
         return remote(bias_s, bias_all.at[p.t], bias_send, bias_recv, step, p.to_z(step))
@@ -486,7 +512,7 @@
             (2, "start"): [(QKV, "t3"), (OUT, "t1 t2")],
             (2, "mid"): [(OUT, "t3")],
             (2, "end"): [(QKV, "a3"), (OUT, "a1 a2 a3"), (UP, "f2")],
-            (3, "start"): [(UP, "s1 f3")],
+            (3, "start"): [(UP, "t1 f3")],
             (3, "end"): [(UP, "s2")],
         }
         for (at, where), plan in plans.items():
@@ -562,7 +588,7 @@
     normed1 = normal1 * gain1_ref[...] + shift1_ref[...]
     hidden_s[...] = normed1.astype(BF)
     acc[...] = normed1 + down_bias_ref[...]
-    relay([(UP, "t1")])
+    relay([(UP, "a1")])
 
     def up_step(step, carry):
         on(step, 0, up_load.wait, up_save.start)
@@ -574,11 +600,11 @@
         act_s[step] = (upper * cdf).astype(BF)
         density = jnp.exp(-0.5 * upper * upper) * 0.3989422804014327
         slope_s[step] = (cdf + upper * density).astype(BF)
-        on(step, 0, lambda: relay([(UP, "a1 s3"), (DOWN, "f1")]))
+        on(step, 0, lambda: relay([(UP, "s3"), (DOWN, "f1")]))
         on(step, 1, up_save.wait, down_load.start)
         on(step, 1, lambda: relay([(UP, "t2"), (DOWN, "f2"), (UP, "t3"), (DOWN, "f3"), (UP, "a2")]))
-        on(step, 2, lambda: relay([(UP, "a3"), (DOWN, "s1")]))
-        on(step, 3, lambda: relay([(DOWN, "s2")]))
+        on(step, 2, lambda: relay([(UP, "a3"), (DOWN, "t1")]))
+        on(step, 3, lambda: relay([(DOWN, "s2 a1")]))
         return carry
 
     lax.fori_loop(0, 4, up_step, 0)
@@ -590,7 +616,7 @@
         for i in (1, 2, 3):
             on(step, i, load_copy(DOWN, i).wait)
         acc[...] += product(act_s[step], w_s[step].reshape(model, model))
-        on(step, 0, lambda: relay([(DOWN, "s3 t1 t2 a1")]))
+        on(step, 0, lambda: relay([(DOWN, "s3 t2")]))
         on(step, 1, lambda: relay([(DOWN, "t3 a2")]))
         on(step, 2, lambda: relay([(DOWN, "a3")]))
         return carry
@@ -946,8 +972,8 @@
             pltpu.VMEM((rows, model), BF),
             pltpu.VMEM((6, 16, model), F32),
             pltpu.VMEM((5, 16, model), F32),
-            dma((24,)),
-            dma((24,)),
+            dma((28,)),
+            dma((28,)),
             dma((4,)),
             dma((4,)),
             dma((14,)),

time: 279 us -> 266 us (0.953)
  Pallas kernels: 278 us -> 264 us
    pallas_call x1, Pallas kernels: 267 us -> 254 us  [run_layer(): pl.pallas_call(layer_kernel, in_specs=[smem, anyw, anyw] + [vmem] * 9 + [...]
where the time goes in v2:
time: 266 us; the launch traced here: 265 us
  Pallas kernels  264 us (99%)
    pallas_call x1, Pallas kernels, run_layer(): pl.pallas_call(layer_kernel, in_specs=[smem, anyw, anyw] + [vmem] * 9 + [...  254 us
    pallas_call x1, Pallas kernels, run_results(): pl.pallas_call(results_kernel, grid=(steps,), in_specs=[tall(rows), tall(...  10.3 us

profile of v2, /device:TPU:0, one launch (start us, length us, event | category | flops | bytes accessed | tf_op | source)
XLA Modules:
  0.0 264.7 jit_solution(16538630787605929117)
XLA Ops:
  0.7 253.5 %layer.1 = (bf16[4,4,2,128,768]{4,3,2,1,0:T(8,128)(2,1)}, bf16[4,4,2,32,1024]{4,3,2,1,0:T(8,128)(2,1)}, bf16[4,4,2,128,1024]{4,3,2,1,0:T(8,128)(2,1)}, bf16[4,4,...) custom-call(s32[2]{0:T(128)} %len_ref.1, ...), custom_call_target="tpu_custom_call" | custom-call | flops 99999997952 | bytes 125829120 | tf_op jit(solution)/shard_map/layer/pallas_call | solution.py:948
  254.2 10.3 %results.1 = (bf16[512,1024]{1,0:T(8,128)(2,1)}, f32[512,1024]{1,0:T(8,128)}, f32[1024,256]{1,0:T(8,128)}, f32[1024,256]{1,0:T(8,128)}, f32[1024,256]{1,0:T(8,12...) custom-call(bf16[512,1024]{1,0:T(8,128)(2,1)} %bitcast.31, ...), custom_call_target="tpu_custom_call" | custom-call | tf_op jit(solution)/shard_map/results/pallas_call | solution.py:1075

commit v3 on v2

--- a/solution.py
+++ b/solution.py
@@ -834,11 +834,8 @@
             fold_sides(4 + at)
             fold_core(7 + at)
             fold_corner(6 + at)
-            if at == 2:
+            if at == 3:
                 start_spread(B_DOWN)
-            if at == 3:
-                back_spreads[B_DOWN].second(0)
-                start_spread(B_UP)
 
         for at in range(4):
             on(i, at, lambda at=at: passed_back(at))
@@ -872,19 +869,21 @@
     fold_sides(8)
     fold_core(11)
     fold_corner(10)
-    end_spread(B_DOWN)
-    back_spreads[B_UP].second(0)
+    back_spreads[B_DOWN].second(0)
+    start_spread(B_UP)
     small_next(0)
     fold_sides(9)
     rows_copy(2).start()
     fold_corner(11)
-    end_spread(B_UP)
+    end_spread(B_DOWN)
+    back_spreads[B_UP].second(0)
     small_next(1)
     fold_sides(10)
     rows_copy(3).start()
     small_next(2)
     fold_sides(11)
     start_spread(B_PROJ)
+    end_spread(B_UP)
     small_next(3)
     back_spreads[B_PROJ].second(0)
     small_next(4)

time: 266 us -> 263 us (0.989)
  Pallas kernels: 264 us -> 261 us
where the time goes in v3:
time: 263 us; the launch traced here: 262 us
  Pallas kernels  261 us (99%)
    pallas_call x1, Pallas kernels, run_layer(): pl.pallas_call(layer_kernel, in_specs=[smem, anyw, anyw] + [vmem] * 9 + [...  251 us
    pallas_call x1, Pallas kernels, run_results(): pl.pallas_call(results_kernel, grid=(steps,), in_specs=[tall(rows), tall(...  10.3 us

profile of v3, /device:TPU:0, one launch (start us, length us, event | category | flops | bytes accessed | tf_op | source)
XLA Modules:
  0.0 262.3 jit_solution(1857013737159120312)
XLA Ops:
  0.7 251.1 %layer.1 = (bf16[4,4,2,128,768]{4,3,2,1,0:T(8,128)(2,1)}, bf16[4,4,2,32,1024]{4,3,2,1,0:T(8,128)(2,1)}, bf16[4,4,2,128,1024]{4,3,2,1,0:T(8,128)(2,1)}, bf16[4,4,...) custom-call(s32[2]{0:T(128)} %len_ref.1, ...), custom_call_target="tpu_custom_call" | custom-call | flops 99999997952 | bytes 125829120 | tf_op jit(solution)/shard_map/layer/pallas_call | solution.py:947
  251.8 10.3 %results.1 = (bf16[512,1024]{1,0:T(8,128)(2,1)}, f32[512,1024]{1,0:T(8,128)}, f32[1024,256]{1,0:T(8,128)}, f32[1024,256]{1,0:T(8,128)}, f32[1024,256]{1,0:T(8,12...) custom-call(bf16[512,1024]{1,0:T(8,128)(2,1)} %bitcast.31, ...), custom_call_target="tpu_custom_call" | custom-call | tf_op jit(solution)/shard_map/results/pallas_call | solution.py:1074
